TPU v7x, 512 devices: a whole 4x8x8 slice. The times are simulated.
512 devices in a mesh: rep: 8 (over z_lo, core), row: 8 (over x, z_hi), col: 8 (over y).
Axes of the slice: x: 4, y: 8, z: 8 (z_hi: 2, z_lo: 4; z = z_hi * 4 + z_lo), core: 2. Of those that a mesh axis runs over, the one named last changes fastest.
Arguments:
- p_vals: bfloat16 [256, 8, 6, 4096], P(('row', 'col'), 'rep'), may hold values from -0.75 to 0.75
- p_cols: int32 [256, 8, 6], P(('row', 'col'), 'rep'), may hold values from 0 to 31, as said below
- f_cols: int32 [256, 8, 8, 2], P(('row', 'col')), may hold values from 0 to 3, as said below
Outputs:
- combined: float32 [256, 8, 8, 2, 4096], P(('row', 'col'), 'rep')
Inputs may be any that keep to these rules, and one draw needn't show every extreme that they name: `p_cols`: within one block row and column tile the 6 entries are distinct. `f_cols`: within one block row, column tile and column group the 2 entries are distinct.
All inputs are finite; a program needn't handle non-finite values.
Results may differ from a plain program's by a relative error of at most 0.007.
Values may be sent and summed in bfloat16 or wider, within the bound.
A program may use at most 128 MiB of HBM per device.

v0:
```python
import math

import jax
import jax.numpy as jnp
from jax import lax
from jax.sharding import PartitionSpec as P

BS = 64


def local(p_vals, p_cols, f_cols):
    rep_count = lax.axis_size("rep")
    col_count = lax.axis_size("col")
    block_rows = p_vals.shape[0]
    slot_count = p_vals.shape[2]
    block_area = p_vals.shape[3]
    filter_count = f_cols.shape[3]
    own_vals = p_vals[:, 0]
    own_cols = p_cols[:, 0]
    row_vals, row_cols, row_filter = (
        lax.all_gather(own_vals, "col", axis=0, tiled=True),
        lax.all_gather(own_cols, "col", axis=0, tiled=True),
        lax.all_gather(f_cols, "col", axis=0, tiled=True),
    )
    col_vals, col_cols = (
        lax.all_gather(own_vals, "row", axis=0, tiled=True),
        lax.all_gather(own_cols, "row", axis=0, tiled=True),
    )
    window = col_vals.shape[0] // rep_count
    column_index = lax.axis_index("col")
    chosen = lax.dynamic_index_in_dim(row_filter, column_index, 2, keepdims=False)
    total_rows = row_vals.shape[0]
    outputs = rep_count * filter_count
    lookup = (jnp.arange(rep_count, dtype=jnp.int32)[None, :, None] * window + chosen).reshape(
        total_rows, outputs
    )
    row_step = math.gcd(total_rows, 8)
    block_count = total_rows // row_step
    row_blocks = row_vals.reshape(block_count, row_step, slot_count, block_area)
    key_blocks = row_cols.reshape(block_count, row_step, slot_count)
    index_blocks = lookup.reshape(block_count, row_step, outputs)

    def partial_block(inputs):
        values, row_keys, wanted = inputs
        picked = col_vals[wanted]
        picked_keys = col_cols[wanted]
        equal_keys = (row_keys[:, None, :, None] == picked_keys[:, :, None, :]).astype(jnp.bfloat16)
        aligned = jnp.einsum(
            "bost,botv->bosv", equal_keys, picked, preferred_element_type=jnp.float32
        ).astype(jnp.bfloat16)
        left_blocks = values.reshape(row_step, slot_count, BS, BS)
        right_blocks = aligned.reshape(row_step, outputs, slot_count, BS, BS)
        return jnp.einsum(
            "bsxy,bosky->boxk", left_blocks, right_blocks, preferred_element_type=jnp.float32
        )

    layers = lax.map(partial_block, (row_blocks, key_blocks, index_blocks))
    layers = layers.reshape(col_count, block_rows, rep_count, filter_count, block_area)
    layer_terms = jnp.transpose(layers, (1, 2, 0, 3, 4)).astype(jnp.bfloat16)
    outgoing = layer_terms.reshape(block_rows, rep_count * col_count, filter_count, block_area)
    incoming = lax.all_to_all(outgoing, ("rep", "col"), split_axis=1, concat_axis=1, tiled=True)
    incoming = incoming.reshape(block_rows, rep_count, col_count, filter_count, block_area)
    summed = jnp.sum(incoming.astype(jnp.float32), axis=1)
    own_filter = lax.dynamic_index_in_dim(f_cols, lax.axis_index("rep"), 1, keepdims=False)
    group_ids = jnp.arange(col_count, dtype=jnp.int32)[None, :, None]
    tile_column = (
        group_ids + own_filter // block_rows * col_count
    ) * block_rows + own_filter % block_rows
    present = (own_cols[:, None, None, :] == tile_column[:, :, :, None]).astype(jnp.bfloat16)
    own_entries = jnp.einsum(
        "rcfs,rsv->rcfv", present, own_vals, preferred_element_type=jnp.float32
    )
    result = 2.0 * own_entries - summed
    return result[:, None]


def solution(mesh):
    return jax.shard_map(
        local,
        mesh=mesh,
        in_specs=(
            P(("row", "col"), "rep", None, None),
            P(("row", "col"), "rep", None),
            P(("row", "col"), None, None, None),
        ),
        out_specs=P(("row", "col"), "rep", None, None, None),
        check_vma=False,
    )
```

profile of v0, /device:TPU:1, one launch (start us, length us, event | category | flops | bytes accessed | tf_op | source)
XLA Modules:
  0.0 493.3 jit_solution(18300841494612685329)
XLA Ops:
  6.5 1.7 copy.63
  8.4 0.7 all-gather.7.cloned.1.call-update
  9.1 0.8 copy.61
  9.8 20.9 %all_gather.16 = s32[32,8,8,2]{2,1,3,0:T(8,128)S(1)} all-gather(s32[4,8,8,2]{2,1,3,0:T(8,128)S(1)} %copy.61), channel_id=1, replica_groups=mesh['rep'=8,'row'=8,'col'=8] {'col'}, dimensions={0}, use_global_device_ids=true | all-gather | bytes 18432 | tf_op jit(solution)/shard_map/all_gather | solution.py:23
  30.7 0.1 constant_dynamic-slice_fusion.1
  30.8 0.2 copy.62
  31.0 0.1 squeeze.22
  31.2 0.1 add.75
  31.3 0.1 broadcast_add_fusion
  31.5 19.3 %all-gather = s32[32,1,6]{2,1,0:T(1,128)S(1)} all-gather(s32[4,1,6]{2,1,0:T(1,128)} %param.6), channel_id=2, replica_groups=mesh['rep'=8,'row'=8,'col'=8] {'col'}, dimensions={0}, use_global_device_ids=true | all-gather | bytes 864 | tf_op jit(solution)/shard_map/all_gather | solution.py:22
  50.8 41.3 %all-gather.1 = s32[32,1,6]{2,1,0:T(1,128)S(1)} all-gather(s32[4,1,6]{2,1,0:T(1,128)} %param.6), channel_id=3, replica_groups=mesh['rep'=8,'row'=8,'col'=8] {'row'}, dimensions={0}, use_global_device_ids=true | all-gather | bytes 864 | tf_op jit(solution)/shard_map/all_gather | solution.py:27
  92.1 2.5 copy.67
  94.6 47.7 %all-gather.7.cloned.1.call-done = bf16[32,1,6,4096]{3,2,1,0:T(8,128)(2,1)} async-done(((bf16[4,1,6,4096]{3,2,1,0:T(8,128)(2,1)}), bf16[32,1,6,4096]{3,2,1,0:T(8,128)(2,1)}) %all-gather.7.cloned.1.call-update) | async-done | bytes 1572880 | tf_op jit(solution)/shard_map/all_gather | solution.py:26
  142.2 189.8 %while.10 = (s32[]{:T(128)}, bf16[4,8,16,64,64]{3,4,2,1,0:T(8,128)(2,1)}, s32[4,8,6]{2,1,0:T(8,128)S(1)}, s32[4,8,16]{2,1,0:T(8,128)S(1)}, s32[32,6]{1,0:T(8,128...) while((s32[]{:T(128)}, bf16[4,8,16,64,64]{3,4,2,1,0:T(8,128)(2,1)}, ...), condition=%wide.region_1.2_spmd, body=%wide.region_0.1_spmd.sunk | while | flops 443553664 | bytes 56510112 | solution.py:57
  142.3 8.1 %gather_fusion = bf16[128,6,4096]{2,1,0:T(8,128)(2,1)} fusion(bf16[32,6,4096]{2,1,0:T(8,128)(2,1)} %get-tuple-element.149, s32[1024]{0:T(1024)S(1)} %pad_clamp_fusion.2), kind=kCustom, calls=%fused_computation.1.clone.1 | custom fusion | bytes 12583424 | tf_op jit(solution)/shard_map/while/body/eval_jaxpr/gather | solution.py:45
  150.5 0.6 gather_fusion.1
  151.1 9.0 %convolution_convert_fusion.2 = bf16[8,16,6,4096]{3,2,1,0:T(8,128)(2,1)} fusion(bf16[8,16,6,4096]{3,2,1,0:T(8,128)(2,1)} %bitcast.77, s32[8,16,6]{2,1,0:T(8,128)S(1)} %bitcast.82, s32[8,6]{1,0:T(8,128)S(1)} %dynamic-slice_bitcast_fusion.2), kind=kOutput, calls=%fused_computation.2.clone.1 | convolution fusion | flops 40899072 | bytes 12586176 | tf_op jit(solution)/shard_map/while/body/eval_jaxpr/bost,botv->bosv/dot_general | solution.py:48
  160.1 19.4 %reshape.158 = bf16[8,16,6,64,64]{4,3,2,1,0:T(8,128)(2,1)} reshape(bf16[8,16,6,4096]{3,2,1,0:T(8,128)(2,1)} %convolution_convert_fusion.2) | data formatting | bytes 12582912 | tf_op jit(solution)/shard_map/while/body/eval_jaxpr/reshape | solution.py:52
  179.6 0.8 reshape.159
  180.4 9.3 %bitcast_dynamic-update-slice_fusion.2 = bf16[4,8,16,64,64]{3,4,2,1,0:T(8,128)(2,1)} fusion(bf16[4,8,16,64,64]{3,4,2,1,0:T(8,128)(2,1)} %get-tuple-element.137, s32[]{:T(128)} %get-tuple-element.136, bf16[8,16,6,64,64]{4,3,2,1,0:T(8,128)(2,1)} %reshape.158, bf16[8,6,64,64]{3,2,0,1:T(8,128)(2,1)S(1)} %reshape.159), kind=kOutput, calls=%fused_computation.3.clone.1 | convolution fusion | flops 402653184 | bytes 17170944 | tf_op jit(solution)/shard_map/while/body/eval_jaxpr/bsxy,bosky->boxk/dot_general | solution.py:53
  189.8 8.1 %gather_fusion = bf16[128,6,4096]{2,1,0:T(8,128)(2,1)} fusion(bf16[32,6,4096]{2,1,0:T(8,128)(2,1)} %get-tuple-element.149, s32[1024]{0:T(1024)S(1)} %pad_clamp_fusion.2), kind=kCustom, calls=%fused_computation.1.clone.1 | custom fusion | bytes 12583424 | tf_op jit(solution)/shard_map/while/body/eval_jaxpr/gather | solution.py:45
  197.9 0.6 gather_fusion.1
  198.5 9.0 %convolution_convert_fusion.2 = bf16[8,16,6,4096]{3,2,1,0:T(8,128)(2,1)} fusion(bf16[8,16,6,4096]{3,2,1,0:T(8,128)(2,1)} %bitcast.77, s32[8,16,6]{2,1,0:T(8,128)S(1)} %bitcast.82, s32[8,6]{1,0:T(8,128)S(1)} %dynamic-slice_bitcast_fusion.2), kind=kOutput, calls=%fused_computation.2.clone.1 | convolution fusion | flops 40899072 | bytes 12586176 | tf_op jit(solution)/shard_map/while/body/eval_jaxpr/bost,botv->bosv/dot_general | solution.py:48
  207.6 19.4 %reshape.158 = bf16[8,16,6,64,64]{4,3,2,1,0:T(8,128)(2,1)} reshape(bf16[8,16,6,4096]{3,2,1,0:T(8,128)(2,1)} %convolution_convert_fusion.2) | data formatting | bytes 12582912 | tf_op jit(solution)/shard_map/while/body/eval_jaxpr/reshape | solution.py:52
  227.0 0.8 reshape.159
  227.8 9.3 %bitcast_dynamic-update-slice_fusion.2 = bf16[4,8,16,64,64]{3,4,2,1,0:T(8,128)(2,1)} fusion(bf16[4,8,16,64,64]{3,4,2,1,0:T(8,128)(2,1)} %get-tuple-element.137, s32[]{:T(128)} %get-tuple-element.136, bf16[8,16,6,64,64]{4,3,2,1,0:T(8,128)(2,1)} %reshape.158, bf16[8,6,64,64]{3,2,0,1:T(8,128)(2,1)S(1)} %reshape.159), kind=kOutput, calls=%fused_computation.3.clone.1 | convolution fusion | flops 402653184 | bytes 17170944 | tf_op jit(solution)/shard_map/while/body/eval_jaxpr/bsxy,bosky->boxk/dot_general | solution.py:53
  237.2 8.1 %gather_fusion = bf16[128,6,4096]{2,1,0:T(8,128)(2,1)} fusion(bf16[32,6,4096]{2,1,0:T(8,128)(2,1)} %get-tuple-element.149, s32[1024]{0:T(1024)S(1)} %pad_clamp_fusion.2), kind=kCustom, calls=%fused_computation.1.clone.1 | custom fusion | bytes 12583424 | tf_op jit(solution)/shard_map/while/body/eval_jaxpr/gather | solution.py:45
  245.3 0.6 gather_fusion.1
  246.0 9.0 %convolution_convert_fusion.2 = bf16[8,16,6,4096]{3,2,1,0:T(8,128)(2,1)} fusion(bf16[8,16,6,4096]{3,2,1,0:T(8,128)(2,1)} %bitcast.77, s32[8,16,6]{2,1,0:T(8,128)S(1)} %bitcast.82, s32[8,6]{1,0:T(8,128)S(1)} %dynamic-slice_bitcast_fusion.2), kind=kOutput, calls=%fused_computation.2.clone.1 | convolution fusion | flops 40899072 | bytes 12586176 | tf_op jit(solution)/shard_map/while/body/eval_jaxpr/bost,botv->bosv/dot_general | solution.py:48
  255.0 19.4 %reshape.158 = bf16[8,16,6,64,64]{4,3,2,1,0:T(8,128)(2,1)} reshape(bf16[8,16,6,4096]{3,2,1,0:T(8,128)(2,1)} %convolution_convert_fusion.2) | data formatting | bytes 12582912 | tf_op jit(solution)/shard_map/while/body/eval_jaxpr/reshape | solution.py:52
  274.4 0.8 reshape.159
  275.3 9.3 %bitcast_dynamic-update-slice_fusion.2 = bf16[4,8,16,64,64]{3,4,2,1,0:T(8,128)(2,1)} fusion(bf16[4,8,16,64,64]{3,4,2,1,0:T(8,128)(2,1)} %get-tuple-element.137, s32[]{:T(128)} %get-tuple-element.136, bf16[8,16,6,64,64]{4,3,2,1,0:T(8,128)(2,1)} %reshape.158, bf16[8,6,64,64]{3,2,0,1:T(8,128)(2,1)S(1)} %reshape.159), kind=kOutput, calls=%fused_computation.3.clone.1 | convolution fusion | flops 402653184 | bytes 17170944 | tf_op jit(solution)/shard_map/while/body/eval_jaxpr/bsxy,bosky->boxk/dot_general | solution.py:53
  284.7 8.1 %gather_fusion = bf16[128,6,4096]{2,1,0:T(8,128)(2,1)} fusion(bf16[32,6,4096]{2,1,0:T(8,128)(2,1)} %get-tuple-element.149, s32[1024]{0:T(1024)S(1)} %pad_clamp_fusion.2), kind=kCustom, calls=%fused_computation.1.clone.1 | custom fusion | bytes 12583424 | tf_op jit(solution)/shard_map/while/body/eval_jaxpr/gather | solution.py:45
  292.8 0.6 gather_fusion.1
  293.4 9.0 %convolution_convert_fusion.2 = bf16[8,16,6,4096]{3,2,1,0:T(8,128)(2,1)} fusion(bf16[8,16,6,4096]{3,2,1,0:T(8,128)(2,1)} %bitcast.77, s32[8,16,6]{2,1,0:T(8,128)S(1)} %bitcast.82, s32[8,6]{1,0:T(8,128)S(1)} %dynamic-slice_bitcast_fusion.2), kind=kOutput, calls=%fused_computation.2.clone.1 | convolution fusion | flops 40899072 | bytes 12586176 | tf_op jit(solution)/shard_map/while/body/eval_jaxpr/bost,botv->bosv/dot_general | solution.py:48
  302.5 19.4 %reshape.158 = bf16[8,16,6,64,64]{4,3,2,1,0:T(8,128)(2,1)} reshape(bf16[8,16,6,4096]{3,2,1,0:T(8,128)(2,1)} %convolution_convert_fusion.2) | data formatting | bytes 12582912 | tf_op jit(solution)/shard_map/while/body/eval_jaxpr/reshape | solution.py:52
  321.9 0.8 reshape.159
  322.7 9.3 %bitcast_dynamic-update-slice_fusion.2 = bf16[4,8,16,64,64]{3,4,2,1,0:T(8,128)(2,1)} fusion(bf16[4,8,16,64,64]{3,4,2,1,0:T(8,128)(2,1)} %get-tuple-element.137, s32[]{:T(128)} %get-tuple-element.136, bf16[8,16,6,64,64]{4,3,2,1,0:T(8,128)(2,1)} %reshape.158, bf16[8,6,64,64]{3,2,0,1:T(8,128)(2,1)S(1)} %reshape.159), kind=kOutput, calls=%fused_computation.3.clone.1 | convolution fusion | flops 402653184 | bytes 17170944 | tf_op jit(solution)/shard_map/while/body/eval_jaxpr/bsxy,bosky->boxk/dot_general | solution.py:53
  332.0 11.4 %copy.68 = bf16[4,8,16,64,64]{4,3,2,1,0:T(8,128)(2,1)} copy(bf16[4,8,16,64,64]{3,4,2,1,0:T(8,128)(2,1)} %get-tuple-element.42) | data formatting | bytes 8388608 | tf_op jit(solution)/shard_map/convert_element_type | solution.py:59
  343.4 14.0 %convert_element_type.21 = bf16[8,4,8,2,4096]{4,3,2,1,0:T(2,128)(2,1)} reshape(bf16[4,8,16,64,64]{4,3,2,1,0:T(8,128)(2,1)} %copy.68) | data formatting | bytes 8388608 | tf_op jit(solution)/shard_map/convert_element_type | solution.py:59
  357.4 5.1 %copy.90 = bf16[4,8,8,2,4096]{4,2,1,3,0:T(8,128)(2,1)S(1)} copy(bf16[4,8,8,2,4096]{4,3,1,0,2:T(2,128)(2,1)} %bitcast.80) | data formatting | bytes 8388608 | tf_op jit(solution)/shard_map/convert_element_type | solution.py:59
  362.5 6.4 %copy.70 = bf16[4,64,2,4096]{3,2,0,1:T(2,128)(2,1)} copy(bf16[4,64,2,4096]{3,1,2,0:T(8,128)(2,1)S(1)} %bitcast.81) | data formatting | bytes 8388608 | tf_op jit(solution)/shard_map/reshape | solution.py:60
  368.8 10.0 %all-to-all-start = ((bf16[4,64,2,4096]{3,2,0,1:T(2,128)(2,1)}), bf16[4,64,2,4096]{3,2,0,1:T(2,128)(2,1)}, u32[]{:S(2)}, u32[]{:S(2)}) async-start(bf16[4,64,2,4096]{3,2,0,1:T(2,128)(2,1)} %copy.70), calls=%async_computation | async-start | bytes 8388608 | tf_op jit(solution)/shard_map/all_to_all | solution.py:61
  378.9 0.7 constant_dynamic-slice_fusion.2
  379.6 96.8 %all-to-all-done = bf16[4,64,2,4096]{3,2,0,1:T(2,128)(2,1)} async-done(((bf16[4,64,2,4096]{3,2,0,1:T(2,128)(2,1)}), bf16[4,64,2,4096]{3,2,0,1:T(2,128)(2,1)}, u32[]{:S(2)}, u32[]{:S(2)}) %all-to-all-start) | async-done | bytes 4194336 | tf_op jit(solution)/shard_map/all_to_all | solution.py:61
  476.4 7.4 %convert_reduce_fusion = f32[4,8,2,4096]{3,2,0,1:T(2,128)S(1)} fusion(bf16[4,8,8,2,4096]{4,3,0,2,1:T(2,128)(2,1)} %bitcast.24), kind=kLoop, calls=%fused_computation.12 | loop fusion | flops 3932160 | bytes 5242880 | tf_op jit(solution)/shard_map/reduce_sum | solution.py:63
  483.8 0.8 fusion.5
  484.6 1.8 copy.72
  (34 shorter events, 0.7 us)
Async XLA Ops:
  6.5 85.6 %all-gather.9.cloned.1.call-start = ((), (), s32[]{:S(2)}) async-start(), calls=%async_computation.2 | async-start | bytes 2359296 | tf_op jit(solution)/shard_map/all_gather | solution.py:21
  8.3 133.9 %all-gather.7.cloned.1.call-start = ((), (), s32[]{:S(2)}) async-start(), calls=%async_computation.1 | async-start | bytes 2359296 | tf_op jit(solution)/shard_map/all_gather | solution.py:26
  368.8 114.9 %copy-start = (bf16[4,1,6,4096]{3,0,2,1:T(4,128)(2,1)S(1)}, bf16[4,1,6,4096]{3,0,2,1:T(4,128)(2,1)}, u32[]{:S(2)}) copy-start(bf16[4,1,6,4096]{3,0,2,1:T(4,128)(2,1)} %param.5) | copy-start | bytes 589828
  368.8 114.9 %copy-start.1 = (s32[4,1,6]{2,1,0:T(1,128)S(1)}, s32[4,1,6]{2,1,0:T(1,128)}, u32[]{:S(2)}) copy-start(s32[4,1,6]{2,1,0:T(1,128)} %param.6) | copy-start | bytes 292
  368.8 107.6 %all-to-all-start = ((bf16[4,64,2,4096]{3,2,0,1:T(2,128)(2,1)}), bf16[4,64,2,4096]{3,2,0,1:T(2,128)(2,1)}, u32[]{:S(2)}, u32[]{:S(2)}) async-start(bf16[4,64,2,4096]{3,2,0,1:T(2,128)(2,1)} %copy.70), calls=%async_computation | async-start | bytes 8388608 | tf_op jit(solution)/shard_map/all_to_all | solution.py:61
Sparse Core Ops, SparseCore 0:
  9.4 45.6 all-gather.8
  58.3 83.8 all-gather.6
where the time goes:
time: 498 us; the launch traced here: 493 us
  local copies, waits for them, and re-layouts  161 us (32%)
  waiting for transfers between devices  145 us (29%)
  blocking collectives  81.5 us (16%)
  matrix products  74.1 us (15%)
  between operations  13.5 us (3%)
  starting transfers between devices  10.1 us (2%)
  other arithmetic  7.51 us (2%)
    all_to_all x1, waiting for transfers between devices, local(): lax.all_to_all(outgoing, ('rep', 'col'), split_axis=1, concat_axis=1, til...  96.8 us
    reshape x4, local copies, waits for them, and re-layouts, partial_block(): right_blocks = aligned.reshape(row_step, outputs, slot_count, BS, BS)  77.6 us
    all_gather x1, waiting for transfers between devices, local(): lax.all_gather(own_vals, 'row', axis=0, tiled=True)  47.7 us
    all_gather x1, blocking collectives, local(): lax.all_gather(own_cols, 'row', axis=0, tiled=True)  41.3 us
    dot_general x4, matrix products, partial_block(): jnp.einsum('bsxy,bosky->boxk', left_blocks, right_blocks, preferred_eleme...  37.2 us
    dot_general x4, matrix products, partial_block(): jnp.einsum('bost,botv->bosv', equal_keys, picked, preferred_element_type=...  36.1 us
    gather x4, local copies, waits for them, and re-layouts, partial_block(): picked = col_vals[wanted]  32.4 us
    convert_element_type x3, local copies, waits for them, and re-layouts, local(): layer_terms = jnp.transpose(layers, (1, 2, 0, 3, 4)).astype(jnp.bfloat16)  30.5 us
  transfers between devices with their start and end apart: 3, of which 2 were waited for; matrix products, arithmetic and copies ran while one was open for 1% of the time, Pallas kernels for 0%

commit v1 on v0

v1 whole, which is shorter than its diff:
```python
import functools

import jax
import jax.numpy as jnp
from jax import lax
from jax.experimental import pallas as pl
from jax.experimental.pallas import tpu as pltpu
from jax.sharding import PartitionSpec as P

MESH = pl.DeviceIdType.MESH
BS = 64
TW = 2 * BS
NT = 12
SEC = 25
NX = 4
NZ = 4
NY = 8
RB = 4
SLOT = 6


def kernel(left_ref, right_ref, meta_ref, out_ref,
           lbuf, rtab, otab, lmv, rmv, lms, rms, wbuf, acc, sbuf, rbuf, ysend, yrecv,
           ssem, lr, lmr, rr, rmr, zs, zr, ys, yr, msem):
    rep = lax.axis_index("rep")
    row = lax.axis_index("row")
    y = lax.axis_index("col")
    core = rep % 2
    zl = rep // 2
    zh = row % 2
    x = row // 2
    sib = rep + 1 - 2 * core
    far_row = row + 1 - 2 * zh
    same = core == zh

    def dev(a, b, c):
        return {"rep": a, "row": b, "col": c}

    yp = (y + 1) % NY
    ym = (y + NY - 1) % NY
    xp = (x + 1) % NX
    xm = (x + NX - 1) % NX
    up, down = dev(rep, row, yp), dev(rep, row, ym)
    sibling = dev(sib, row, y)
    xright, xleft = dev(rep, xp * 2 + zh, y), dev(rep, xm * 2 + zh, y)

    partners = [sibling, dev(rep, far_row, y), dev(sib, far_row, y), xright, xleft]
    partners += [dev(rep, row, (y + s) % NY) for s in range(1, NY)]
    partners += [dev((zl + 1) % NZ * 2 + core, row, y), dev((zl + NZ - 1) % NZ * 2 + core, row, y)]
    barrier = pltpu.get_barrier_semaphore()
    for p in partners:
        pl.semaphore_signal(barrier, inc=1, device_id=p, device_id_type=MESH)
    pl.semaphore_wait(barrier, len(partners))

    counter = [0]
    sent = []

    def describe(i, src, dst, rsem, to):
        return pltpu.make_async_remote_copy(
            src_ref=src, dst_ref=dst, send_sem=ssem.at[i], recv_sem=rsem,
            device_id=to, device_id_type=MESH)

    def send(src, dst, rsem, to):
        i = counter[0]
        counter[0] += 1
        describe(i, src, dst, rsem, to).start()
        sent.append((i, src, dst, rsem, to))

    def arrive(dst, rsem):
        pltpu.make_async_remote_copy(
            src_ref=dst, dst_ref=dst, send_sem=ssem.at[0], recv_sem=rsem,
            device_id=sibling, device_id_type=MESH).wait_recv()

    def lslot(yy, t):
        return yy * 2 + t

    def ltiles(s, half=None):
        if half is None:
            return lbuf.at[pl.ds(s * NT, NT)]
        return lbuf.at[pl.ds(s * NT + half * (NT // 2), NT // 2)]

    def rtiles(s):
        return rtab.at[pl.ds(s * SEC, NT)]

    own = lslot(y, core)
    own_sec = x * 2 + core
    send(right_ref, rtiles(own_sec), rr.at[own_sec], dev(zl * 2 + zh, far_row, y))
    send(meta_ref, rmv.at[own_sec], rmr.at[own_sec], dev(zl * 2 + zh, far_row, y))
    sib_mark = counter[0]
    counter[0] += 2

    def to_sibling():
        return (describe(sib_mark, right_ref, rtiles(own_sec), rr.at[own_sec], sibling),
                describe(sib_mark + 1, meta_ref, rmv.at[own_sec], rmr.at[own_sec], sibling))

    @pl.when(jnp.logical_not(same))
    def _():
        for c in to_sibling():
            c.start()

    for to in (up, down, sibling):
        send(left_ref, ltiles(own), lr.at[own, 0], to)
        send(meta_ref, lmv.at[own], lmr.at[own], to)

    lbuf[pl.ds(own * NT, NT)] = left_ref[...]
    lmv[own] = meta_ref[...]
    zero_tile = jnp.zeros((BS, TW), jnp.bfloat16)
    for s in range(2 * NX):
        rtab[s * SEC + 2 * NT] = zero_tile
    otab[2 * NT] = zero_tile

    def swap(v):
        return jnp.concatenate([v[:, BS:], v[:, :BS]], axis=1)

    otab[pl.ds(0, NT)] = left_ref[...]

    def own_swap(i, carry):
        otab[NT + i] = swap(left_ref[i])
        return carry

    lax.fori_loop(0, NT, own_swap, 0)

    base_mark = counter[0]
    counter[0] += 8

    def xcopies():
        i = base_mark
        for t in range(2):
            sec = x * 2 + t
            for to in ((xright, xleft) if t == 0 else (xleft, xright)):
                yield describe(i, rtiles(sec), rtiles(sec), rr.at[sec], to)
                yield describe(i + 1, rmv.at[sec], rmv.at[sec], rmr.at[sec], to)
                i += 2

    def base(first):
        other_sec = x * 2 + 1 - core
        if first:
            rtab[pl.ds(own_sec * SEC, NT)] = right_ref[...]
            rmv[own_sec] = meta_ref[...]
        else:
            arrive(rtiles(own_sec), rr.at[own_sec])
            arrive(rmv.at[own_sec], rmr.at[own_sec])
        arrive(rtiles(other_sec), rr.at[other_sec])
        arrive(rmv.at[other_sec], rmr.at[other_sec])
        for c in xcopies():
            c.start()

    @pl.when(same)
    def _():
        base(True)

    def lstep(s):
        a = lslot((y + NY - s) % NY, core)
        b = lslot((y + s) % NY, core)
        for slot, to, half in ((a, up, 0), (b, down, 1)):
            arrive(ltiles(slot), lr.at[slot, 0])
            if s < 3:
                send(ltiles(slot), ltiles(slot), lr.at[slot, 0], to)
            else:
                send(ltiles(slot, half), ltiles(slot, half), lr.at[slot, half], to)
            send(ltiles(slot), ltiles(slot), lr.at[slot, 0], sibling)
            arrive(lmv.at[slot], lmr.at[slot])
            if s < 3 or half == 0:
                send(lmv.at[slot], lmv.at[slot], lmr.at[slot], to)
            send(lmv.at[slot], lmv.at[slot], lmr.at[slot], sibling)

    lstep(1)
    lstep(2)

    @pl.when(jnp.logical_not(same))
    def _():
        base(False)

    lstep(3)

    def rhop(src_x, t, to):
        sec = src_x * 2 + t
        arrive(rtiles(sec), rr.at[sec])
        arrive(rmv.at[sec], rmr.at[sec])
        if to is not None:
            send(rtiles(sec), rtiles(sec), rr.at[sec], to)
            send(rmv.at[sec], rmv.at[sec], rmr.at[sec], to)

    rhop(xm, 0, xright)
    rhop(xp, 1, xleft)
    rhop(xm, 1, None)
    rhop(xp, 0, None)

    far = lslot((y + 4) % NY, core)
    for half in range(2):
        arrive(ltiles(far, half), lr.at[far, half])
        send(ltiles(far, half), ltiles(far, half), lr.at[far, half], sibling)
    arrive(lmv.at[far], lmr.at[far])
    send(lmv.at[far], lmv.at[far], lmr.at[far], sibling)

    def widen(xx):
        def body(i, carry):
            first = xx * 2 * SEC + i
            rtab[first + NT] = swap(rtab[first])
            rtab[first + SEC + NT] = swap(rtab[first + SEC])
            return carry
        lax.fori_loop(0, NT, body, 0)

    widen(x)
    widen(xm)
    widen(xp)
    x2 = (x + 2) % NX
    rhop(x2, 0, None)
    rhop(x2, 1, None)
    widen(x2)

    rm_copy = pltpu.make_async_copy(rmv, rms, msem.at[0])
    rm_copy.start()
    for s in range(NY):
        slot = lslot((y + s) % NY, 1 - core)
        arrive(lmv.at[slot], lmr.at[slot])
    lm_copy = pltpu.make_async_copy(lmv, lms, msem.at[1])
    lm_copy.start()
    for s in range(NY):
        slot = lslot((y + s) % NY, 1 - core)
        if s == 4:
            for half in range(2):
                arrive(ltiles(slot, half), lr.at[slot, half])
        else:
            arrive(ltiles(slot), lr.at[slot, 0])
    rm_copy.wait()
    lm_copy.wait()

    lane = lax.broadcasted_iota(jnp.int32, (BS, TW), 1)
    low = lane < BS

    def group_of(n):
        away = (n + 1) // 2
        return (y + jnp.where(n % 2 == 1, NY - away, away)) % NY

    def compute(n):
        g = group_of(n)
        for rb in range(RB):
            tiles = []
            for t in range(2):
                for pair in range(3):
                    tiles.append(lbuf[(g * 2 + t) * NT + rb * 3 + pair])
            lhs = jnp.concatenate(tiles, axis=1)
            keys = [lms[g * 2 + t, 6, rb * SLOT + s] for t in range(2) for s in range(SLOT)]
            for d in range(NZ):
                at = (2 * d + core) * 16 + y * 2
                j0 = lms[g * 2, rb, at] * 32
                j1 = lms[g * 2, rb, at + 1] * 32
                for t in range(2):
                    sec = d * 2 + t
                    for s in range(SLOT):
                        k = keys[t * SLOT + s]
                        lo = rtab[sec * SEC + rms[sec, 4, j0 + k]]
                        hi = rtab[sec * SEC + rms[sec, 5, j1 + k]]
                        wbuf[rb % 2, pl.ds((t * SLOT + s) * BS, BS), pl.ds(d * TW, TW)] = jnp.where(low, lo, hi)
            res = jnp.dot(lhs, wbuf[rb % 2], preferred_element_type=jnp.float32)
            for d in range(NZ):
                acc[n * NZ + d, pl.ds(rb * BS, BS), :] = res[:, d * TW:(d + 1) * TW]

    def zcopy(n, d):
        right = d > zl
        side = jnp.where(right, 0, 1)
        nxt = jnp.where(right, zl + 1, zl - 1)
        return pltpu.make_async_remote_copy(
            src_ref=sbuf.at[n * NZ + d], dst_ref=rbuf.at[side, n * NZ + d],
            send_sem=zs.at[n * NZ + d], recv_sem=zr.at[side, n * NZ + d],
            device_id=dev(nxt * 2 + core, row, y), device_id_type=MESH)

    def reduce_on(n):
        for step in range(NZ):
            d = jnp.where(zl < 2, NZ - 1 - step, step)
            right = d > zl
            side = jnp.where(right, 0, 1)
            hears = jnp.logical_or(jnp.logical_and(right, zl > 0), jnp.logical_and(d < zl, zl < NZ - 1))

            @pl.when(d != zl)
            def _():
                @pl.when(hears)
                def _():
                    arrive(rbuf.at[side, n * NZ + d], zr.at[side, n * NZ + d])
                    sbuf[n * NZ + d] = (acc[n * NZ + d] + rbuf[side, n * NZ + d].astype(jnp.float32)).astype(jnp.bfloat16)

                @pl.when(jnp.logical_not(hears))
                def _():
                    sbuf[n * NZ + d] = acc[n * NZ + d].astype(jnp.bfloat16)

                zcopy(n, d).start()

    def ycopy(n):
        return pltpu.make_async_remote_copy(
            src_ref=ysend.at[n], dst_ref=yrecv.at[y], send_sem=ys.at[n], recv_sem=yr.at[y],
            device_id=dev(rep, row, group_of(n)), device_id_type=MESH)

    def finish(n):
        at = n * NZ + zl

        @pl.when(zl > 0)
        def _():
            arrive(rbuf.at[0, at], zr.at[0, at])
            acc[at] = acc[at] + rbuf[0, at].astype(jnp.float32)

        @pl.when(zl < NZ - 1)
        def _():
            arrive(rbuf.at[1, at], zr.at[1, at])
            acc[at] = acc[at] + rbuf[1, at].astype(jnp.float32)

        total = acc[at].astype(jnp.bfloat16)

        @pl.when(n == 0)
        def _():
            yrecv[y] = total

        @pl.when(n > 0)
        def _():
            ysend[n] = total
            ycopy(n).start()

    def main(n, carry):
        @pl.when(n < NY)
        def _():
            compute(n)
            reduce_on(n)

        @pl.when(n >= 2)
        def _():
            finish(n - 2)
        return carry

    lax.fori_loop(0, NY + 2, main, 0)

    par = lax.broadcasted_iota(jnp.int32, (BS, TW), 0) % 2
    half_of = lane // BS

    def combine(s, carry):
        c = group_of(s)

        @pl.when(s > 0)
        def _():
            arrive(yrecv.at[c], yr.at[c])

        for rb in range(RB):
            at = rep * 16 + c * 2
            k0 = rb * 32 + c * RB + lms[own, rb, at]
            k1 = rb * 32 + c * RB + lms[own, rb, at + 1]
            mine = jnp.where(low, otab[lms[own, 4, k0]].astype(jnp.float32), otab[lms[own, 5, k1]].astype(jnp.float32))
            m = 2.0 * mine - yrecv[c, pl.ds(rb * BS, BS), :].astype(jnp.float32)
            turned = pltpu.roll(m, BS, 1)
            out_ref[rb * NY + c] = jnp.where(
                par == half_of, m,
                jnp.where(par == 0, pltpu.roll(turned, BS - 1, 0), pltpu.roll(turned, 1, 0)))
        return carry

    lax.fori_loop(0, NY, combine, 0)

    for c in sent:
        describe(*c).wait_send()
    for c in xcopies():
        c.wait_send()

    @pl.when(jnp.logical_not(same))
    def _():
        for c in to_sibling():
            c.wait_send()

    def drain(n, carry):
        for d in range(NZ):
            @pl.when(zl != d)
            def _():
                zcopy(n, d).wait_send()

        @pl.when(n > 0)
        def _():
            ycopy(n).wait_send()
        return carry

    lax.fori_loop(0, NY, drain, 0)


def local(p_vals, p_cols, f_cols):
    vals = p_vals.reshape(RB, 3, 2, BS, BS)
    left = vals.transpose(0, 1, 3, 2, 4).reshape(NT, BS, TW)
    right = vals.transpose(0, 1, 4, 2, 3).reshape(NT, BS, TW)
    keys = p_cols[:, 0]
    slot = jnp.arange(SLOT, dtype=jnp.int32)[None]
    place = jnp.arange(RB, dtype=jnp.int32)[:, None] * 3 + slot // 2
    hit = keys[:, None, :] == jnp.arange(32, dtype=jnp.int32)[None, :, None]
    lo = jnp.min(jnp.where(hit, (place + slot % 2 * NT)[:, None], 2 * NT), axis=2)
    hi = jnp.min(jnp.where(hit, (place + (1 - slot % 2) * NT)[:, None], 2 * NT), axis=2)
    meta = jnp.concatenate([
        f_cols.reshape(RB, 128), lo.reshape(1, 128), hi.reshape(1, 128),
        jnp.pad(keys.reshape(1, RB * SLOT), ((0, 1), (0, 128 - RB * SLOT)))], axis=0)

    vm = pl.BlockSpec(memory_space=pltpu.VMEM)
    bf, f32 = jnp.bfloat16, jnp.float32
    out = pl.pallas_call(
        kernel,
        out_shape=jax.ShapeDtypeStruct((RB * NY, BS, TW), f32),
        in_specs=[vm] * 3,
        out_specs=vm,
        scratch_shapes=[
            pltpu.VMEM((2 * NY * NT, BS, TW), bf),
            pltpu.VMEM((2 * NX * SEC, BS, TW), bf),
            pltpu.VMEM((SEC, BS, TW), bf),
            pltpu.VMEM((2 * NY, 8, 128), jnp.int32),
            pltpu.VMEM((2 * NX, 8, 128), jnp.int32),
            pltpu.SMEM((2 * NY, 8, 128), jnp.int32),
            pltpu.SMEM((2 * NX, 8, 128), jnp.int32),
            pltpu.VMEM((2, 2 * SLOT * BS, NZ * TW), bf),
            pltpu.VMEM((NY * NZ, RB * BS, TW), f32),
            pltpu.VMEM((NY * NZ, RB * BS, TW), bf),
            pltpu.VMEM((2, NY * NZ, RB * BS, TW), bf),
            pltpu.VMEM((NY, RB * BS, TW), bf),
            pltpu.VMEM((NY, RB * BS, TW), bf),
            pltpu.SemaphoreType.DMA((64,)),
            pltpu.SemaphoreType.DMA((2 * NY, 2)),
            pltpu.SemaphoreType.DMA((2 * NY,)),
            pltpu.SemaphoreType.DMA((2 * NX,)),
            pltpu.SemaphoreType.DMA((2 * NX,)),
            pltpu.SemaphoreType.DMA((NY * NZ,)),
            pltpu.SemaphoreType.DMA((2, NY * NZ)),
            pltpu.SemaphoreType.DMA((NY,)),
            pltpu.SemaphoreType.DMA((NY,)),
            pltpu.SemaphoreType.DMA((2,)),
        ],
        compiler_params=pltpu.CompilerParams(
            collective_id=0, has_side_effects=True, vmem_limit_bytes=48 * 1024 * 1024),
    )(left, right, meta)
    out = out.reshape(RB, NY, BS // 2, 2, TW).transpose(0, 1, 3, 2, 4)
    return out.reshape(RB, 1, NY, 2, BS * BS)


def solution(mesh):
    return jax.shard_map(
        local,
        mesh=mesh,
        in_specs=(
            P(("row", "col"), "rep", None, None),
            P(("row", "col"), "rep", None),
            P(("row", "col"), None, None, None),
        ),
        out_specs=P(("row", "col"), "rep", None, None, None),
        check_vma=False,
    )
```

time: 498 us -> 104 us (0.21)
  the two profiles are of different devices: /device:TPU:1 before, /device:TPU:2 now
where the time goes in v1:
time: 104 us
  Pallas kernels  98.3 us (95%)
  local copies, waits for them, and re-layouts  4.28 us (4%)
  other arithmetic  1.55 us (1%)
    pallas_call x1, Pallas kernels, local(): pl.pallas_call(kernel, out_shape=jax.ShapeDtypeStruct((RB * NY, BS, TW),...  98.3 us

profile of v1, /device:TPU:2, one launch (start us, length us, event | category | flops | bytes accessed | tf_op | source)
XLA Modules:
  0.0 104.2 jit_solution(14666958714863042412)
XLA Ops:
  0.0 0.0 copy-start.1
  0.0 0.0 copy-start
  0.0 0.5 broadcast.165
  0.5 1.3 %reduce.3 = s32[4,6]{1,0:T(4,128)S(1)} reduce(s32[4,1,6]{2,1,0:T(1,128)} %param.4, s32[]{:T(128)} %broadcast.165), dimensions={1}, to_apply=%param.4.reduce_sub_computation.3 | reduce | bytes 196 | tf_op args[1]
  1.9 0.1 reshape_squeeze.3
  2.0 0.8 copy.16
  2.7 0.1 add_add_fusion
  2.8 0.1 select_reduce_fusion.1
  2.9 0.1 reshape.161
  3.0 0.1 reshape.162
  3.1 0.0 copy-done.1
  3.1 0.2 copy.15
  3.3 0.1 copy.17
  3.4 0.0 copy-done
  3.4 0.4 reshape.157
  3.7 0.4 copy.14
  4.1 0.4 copy.20
  4.5 0.2 reshape.158.left_ref
  4.7 0.2 reshape.159.right_ref
  4.9 98.3 %shard_map.37 = f32[32,64,128]{2,1,0:T(8,128)S(1)} custom-call(bf16[12,64,128]{2,1,0:T(8,128)(2,1)S(1)} %reshape.158.left_ref, bf16[12,64,128]{2,1,0:T(8,128)(2,1)S(1)} %reshape.159.right_ref, s32[8,128]{1,0:T(8,128)S(1)} %pad_add_fusion.meta_ref), custom_call_target="tpu_custom_call" | custom-call | tf_op jit(solution)/shard_map/pallas_call | solution.py:395
  103.2 1.0 copy.22
  (4 shorter events, 0.0 us)
Async XLA Ops:
  0.0 3.1 %copy-start.1 = (s32[4,8,8,2]{2,3,1,0:T(2,128)S(1)}, s32[4,8,8,2]{2,3,1,0:T(2,128)}, u32[]{:S(2)}) copy-start(s32[4,8,8,2]{2,3,1,0:T(2,128)} %param.5) | copy-start | bytes 6148
  0.0 3.4 %copy-start = (bf16[4,1,6,4096]{3,0,2,1:T(4,128)(2,1)S(1)}, bf16[4,1,6,4096]{3,0,2,1:T(4,128)(2,1)}, u32[]{:S(2)}) copy-start(bf16[4,1,6,4096]{3,0,2,1:T(4,128)(2,1)} %param.3) | copy-start | bytes 589828

commit v2 on v0

v2 whole, which is shorter than its diff:
```python
import functools

import jax
import jax.numpy as jnp
from jax import lax
from jax.experimental import pallas as pl
from jax.experimental.pallas import tpu as pltpu
from jax.sharding import PartitionSpec as P

MESH = pl.DeviceIdType.MESH
BS = 64
TW = 2 * BS
NT = 12
SEC = 25
NX = 4
NZ = 4
NY = 8
RB = 4
SLOT = 6
LAG = 2


def kernel(left_ref, right_ref, meta_ref, out_ref,
           lbuf, rtab, otab, lmv, rmv, lms, rms, oms, wbuf, keep, sbuf, rbuf, ysend, yrecv,
           ssem, lr, lmr, rr, rmr, zs, zr, ys, yr, msem):
    rep = lax.axis_index("rep")
    row = lax.axis_index("row")
    y = lax.axis_index("col")
    core = rep % 2
    zl = rep // 2
    zh = row % 2
    x = row // 2
    zp = zl % 2
    other = 1 - core
    zn = zl + 1 - 2 * zp
    zf = (zl + 2) % NZ
    far_row = row + 1 - 2 * zh
    is_base = x % 2 == zp
    same = core == zh
    keeps_own = jnp.logical_and(is_base, same)

    def dev(a, b, c):
        return {"rep": a, "row": b, "col": c}

    xp = (x + 1) % NX
    xm = (x + NX - 1) % NX
    up, down = dev(rep, row, (y + 1) % NY), dev(rep, row, (y + NY - 1) % NY)
    sibling = dev(zl * 2 + other, row, y)
    z_next = dev(zn * 2 + core, row, y)
    z_far = dev(zf * 2 + core, row, y)
    xright, xleft = dev(rep, xp * 2 + zh, y), dev(rep, xm * 2 + zh, y)

    partners = [xright, xleft, z_far]
    for r in (row, far_row):
        for z in (zl, zn):
            for c in (core, other):
                if not (r is row and z is zl and c is core):
                    partners.append(dev(z * 2 + c, r, y))
    partners += [dev(rep, row, (y + s) % NY) for s in range(1, NY)]
    barrier = pltpu.get_barrier_semaphore()
    for p in partners:
        pl.semaphore_signal(barrier, inc=1, device_id=p, device_id_type=MESH)
    pl.semaphore_wait(barrier, len(partners))

    counter = [0]
    sent = []

    def describe(i, src, dst, rsem, to):
        return pltpu.make_async_remote_copy(
            src_ref=src, dst_ref=dst, send_sem=ssem.at[i], recv_sem=rsem,
            device_id=to, device_id_type=MESH)

    def take(count):
        first = counter[0]
        counter[0] += count
        return first

    def send(src, dst, rsem, to):
        i = take(1)
        describe(i, src, dst, rsem, to).start()
        sent.append((i, src, dst, rsem, to))

    def arrive(dst, rsem):
        pltpu.make_async_remote_copy(
            src_ref=dst, dst_ref=dst, send_sem=ssem.at[0], recv_sem=rsem,
            device_id=sibling, device_id_type=MESH).wait_recv()

    def lslot(yy, c, q):
        return (yy * 2 + c) * 2 + q

    def ltiles(s):
        return lbuf.at[pl.ds(s * NT, NT)]

    def rtiles(s):
        return rtab.at[pl.ds(s * SEC, NT)]

    def rsec(xx, c, q):
        return xx // 2 * 4 + c * 2 + q

    own = lslot(y, core, zp)
    own_sec = rsec(x, core, zp)
    zt = jnp.where(is_base, zl, zn)
    base_far = dev(zt * 2 + zh, far_row, y)
    base_near = dev(zt * 2 + zh, row, y)
    near_mark = take(2)

    def near_copies():
        return (describe(near_mark, right_ref, rtiles(own_sec), rr.at[own_sec], base_near),
                describe(near_mark + 1, meta_ref, rmv.at[own_sec], rmr.at[own_sec], base_near))

    send(right_ref, rtiles(own_sec), rr.at[own_sec], base_far)
    send(meta_ref, rmv.at[own_sec], rmr.at[own_sec], base_far)

    @pl.when(jnp.logical_not(keeps_own))
    def _():
        for c in near_copies():
            c.start()

    def lsend(src, msrc, slot, to):
        send(src, ltiles(slot), lr.at[slot], to)
        send(msrc, lmv.at[slot], lmr.at[slot], to)

    for to in (z_next, up, down, sibling):
        lsend(left_ref, meta_ref, own, to)

    order = [(core, zp), (other, zp), (core, 1 - zp), (other, 1 - zp)]
    base_mark = take(16)

    def xcopies(k):
        sec = rsec(x, *order[k])
        i = base_mark + 4 * k
        for to in ((xright, xleft) if k % 2 == 0 else (xleft, xright)):
            yield describe(i, rtiles(sec), rtiles(sec), rr.at[sec], to)
            yield describe(i + 1, rmv.at[sec], rmv.at[sec], rmr.at[sec], to)
            i += 2

    def rarrive(sec):
        arrive(rtiles(sec), rr.at[sec])
        arrive(rmv.at[sec], rmr.at[sec])

    def base(ks):
        for k in ks:
            rarrive(rsec(x, *order[k]))
            for c in xcopies(k):
                c.start()

    @pl.when(keeps_own)
    def _():
        rtab[pl.ds(own_sec * SEC, NT)] = right_ref[...]
        rmv[own_sec] = meta_ref[...]
        for c in xcopies(0):
            c.start()

    lbuf[pl.ds(own * NT, NT)] = left_ref[...]
    lmv[own] = meta_ref[...]
    zero_tile = jnp.zeros((BS, TW), jnp.bfloat16)
    for s in range(8):
        rtab[s * SEC + 2 * NT] = zero_tile
    otab[2 * NT] = zero_tile

    def swap(v):
        return jnp.concatenate([v[:, BS:], v[:, :BS]], axis=1)

    for i in range(NT):
        v = left_ref[i]
        otab[i] = v
        otab[NT + i] = swap(v)

    def larrive(slot):
        arrive(ltiles(slot), lr.at[slot])
        arrive(lmv.at[slot], lmr.at[slot])

    def lpass(slot, to):
        lsend(ltiles(slot), lmv.at[slot], slot, to)

    marks = {1: take(16), 2: take(16), 3: take(12), 4: take(4)}

    def lring(s):
        i = marks[s]
        for q, half in ((zp, 0), (1 - zp, 1)):
            for yy, to, way in (((y + NY - s) % NY, up, 0), ((y + s) % NY, down, 1)):
                if s == 4 and way == 1:
                    continue
                slot = lslot(yy, core, q)
                goals = [to] if s < 3 or (s == 3 and half == way) else []
                copies = []
                for goal in goals + [sibling]:
                    copies.append(describe(i, ltiles(slot), ltiles(slot), lr.at[slot], goal))
                    copies.append(describe(i + 1, lmv.at[slot], lmv.at[slot], lmr.at[slot], goal))
                    i += 2
                yield slot, copies

    def lstep(s):
        for slot, copies in lring(s):
            larrive(slot)
            for c in copies:
                c.start()

    hop_mark = take(8)

    def hops(k):
        sec = rsec(xm if k % 2 == 0 else xp, *order[k])
        to = xright if k % 2 == 0 else xleft
        return (sec, describe(hop_mark + 2 * k, rtiles(sec), rtiles(sec), rr.at[sec], to),
                describe(hop_mark + 2 * k + 1, rmv.at[sec], rmv.at[sec], rmr.at[sec], to))

    def hop_on(ks):
        for k in ks:
            sec, a, b = hops(k)
            rarrive(sec)
            a.start()
            b.start()

    no_base = jnp.logical_not(is_base)
    differs = jnp.logical_not(same)

    @pl.when(keeps_own)
    def _():
        base((1, 2, 3))

    pair = lslot(y, core, 1 - zp)
    larrive(pair)
    for to in (up, down, sibling):
        lpass(pair, to)

    @pl.when(jnp.logical_and(is_base, differs))
    def _():
        base((0, 1, 2, 3))

    @pl.when(jnp.logical_and(no_base, same))
    def _():
        hop_on((0, 1, 2, 3))

    lstep(1)

    @pl.when(jnp.logical_and(no_base, differs))
    def _():
        hop_on((0, 1))

    @pl.when(differs)
    def _():
        lstep(2)

    @pl.when(jnp.logical_and(no_base, differs))
    def _():
        hop_on((2, 3))

    @pl.when(no_base)
    def _():
        for k in range(4):
            rarrive(rsec(xp if k % 2 == 0 else xm, *order[k]))

    @pl.when(is_base)
    def _():
        for k in range(4):
            rarrive(rsec((x + 2) % NX, *order[k]))

    rm_copy = pltpu.make_async_copy(rmv, rms, msem.at[0])
    rm_copy.start()
    om_copy = pltpu.make_async_copy(meta_ref, oms, msem.at[2])
    om_copy.start()

    def widen(sec, carry):
        for i in range(NT):
            rtab[sec * SEC + NT + i] = swap(rtab[sec * SEC + i])
        return carry

    lax.fori_loop(0, 8, widen, 0)

    lane = lax.broadcasted_iota(jnp.int32, (BS, TW), 1)
    low = lane < BS

    def group_of(n):
        away = (n + 1) // 2
        return (y + jnp.where(n % 2 == 1, NY - away, away)) % NY

    def meta_copy(n):
        g = group_of(n)
        return pltpu.make_async_copy(lmv.at[pl.ds(g * 4, 4)], lms.at[pl.ds(g * 4, 4)], msem.at[1])

    def meta_in(n):
        g = group_of(n)
        for q in range(2):
            slot = lslot(g, other, q)
            arrive(lmv.at[slot], lmr.at[slot])
        meta_copy(n).start()

    def compute(n):
        g = group_of(n)
        for q in range(2):
            slot = lslot(g, other, q)
            arrive(ltiles(slot), lr.at[slot])
        dests = (zl, zf)
        for rb in range(RB):
            tiles = [lbuf[(g * 4 + t) * NT + rb * 3 + p] for t in range(4) for p in range(3)]
            lhs = jnp.concatenate(tiles, axis=1)
            keys = [lms[g * 4 + t, 4 + rb, 64 + s] for t in range(4) for s in range(SLOT)]
            for i, d in enumerate(dests):
                at = (2 * d + core) * 16 + y * 2
                j0 = lms[g * 4, rb, at] + 4
                j1 = lms[g * 4, rb, at + 1] + 4
                for t in range(4):
                    sec = d // 2 * 4 + t
                    for s in range(SLOT):
                        k = keys[t * SLOT + s]
                        lo = rtab[sec * SEC + rms[sec, j0, k]]
                        hi = rtab[sec * SEC + rms[sec, j1, k + 32]]
                        wbuf[rb % 2, pl.ds((t * SLOT + s) * BS, BS), pl.ds(i * TW, TW)] = jnp.where(low, lo, hi)
            res = jnp.dot(lhs, wbuf[rb % 2], preferred_element_type=jnp.float32)
            keep[n, pl.ds(rb * BS, BS), :] = res[:, :TW]
            sbuf[n, pl.ds(rb * BS, BS), :] = res[:, TW:].astype(jnp.bfloat16)

    def zcopy(n):
        return pltpu.make_async_remote_copy(
            src_ref=sbuf.at[n], dst_ref=rbuf.at[n], send_sem=zs.at[n], recv_sem=zr.at[n],
            device_id=z_far, device_id_type=MESH)

    def ycopy(n):
        return pltpu.make_async_remote_copy(
            src_ref=ysend.at[n], dst_ref=yrecv.at[y], send_sem=ys.at[n], recv_sem=yr.at[y],
            device_id=dev(rep, row, group_of(n)), device_id_type=MESH)

    def finish(n):
        arrive(rbuf.at[n], zr.at[n])
        total = (keep[n] + rbuf[n].astype(jnp.float32)).astype(jnp.bfloat16)

        @pl.when(n == 0)
        def _():
            yrecv[y] = total

        @pl.when(n > 0)
        def _():
            ysend[n] = total
            ycopy(n).start()

    par = lax.broadcasted_iota(jnp.int32, (BS, TW), 0) % 2
    half_of = lane // BS

    def combine(s):
        c = group_of(s)

        @pl.when(s > 0)
        def _():
            arrive(yrecv.at[c], yr.at[c])

        for rb in range(RB):
            at = rep * 16 + c * 2
            k0 = c * RB + oms[rb, at]
            k1 = 32 + c * RB + oms[rb, at + 1]
            mine = jnp.where(low, otab[oms[4 + rb, k0]].astype(jnp.float32),
                             otab[oms[4 + rb, k1]].astype(jnp.float32))
            m = 2.0 * mine - yrecv[c, pl.ds(rb * BS, BS), :].astype(jnp.float32)
            turned = pltpu.roll(m, BS, 1)
            out_ref[rb * NY + c] = jnp.where(
                par == half_of, m,
                jnp.where(par == 0, pltpu.roll(turned, BS - 1, 0), pltpu.roll(turned, 1, 0)))

    meta_in(0)
    rm_copy.wait()
    om_copy.wait()

    def main(n, carry):
        @pl.when(n < NY)
        def _():
            meta_copy(n).wait()

            @pl.when(jnp.logical_and(n == 1, same))
            def _():
                lstep(2)

            @pl.when(n == 3)
            def _():
                lstep(3)

            @pl.when(n == 5)
            def _():
                lstep(4)

            @pl.when(n < NY - 1)
            def _():
                meta_in(n + 1)

            compute(n)
            zcopy(n).start()

        @pl.when(jnp.logical_and(n >= LAG, n < NY + LAG))
        def _():
            finish(n - LAG)

        @pl.when(n >= 2 * LAG)
        def _():
            combine(n - 2 * LAG)
        return carry

    lax.fori_loop(0, NY + 2 * LAG, main, 0)

    for c in sent:
        describe(*c).wait_send()
    for s in range(1, 5):
        for slot, copies in lring(s):
            for c in copies:
                c.wait_send()

    @pl.when(jnp.logical_not(keeps_own))
    def _():
        for c in near_copies():
            c.wait_send()

    @pl.when(is_base)
    def _():
        for k in range(4):
            for c in xcopies(k):
                c.wait_send()

    @pl.when(jnp.logical_not(is_base))
    def _():
        for k in range(4):
            sec, a, b = hops(k)
            a.wait_send()
            b.wait_send()

    def drain(n, carry):
        zcopy(n).wait_send()

        @pl.when(n > 0)
        def _():
            ycopy(n).wait_send()
        return carry

    lax.fori_loop(0, NY, drain, 0)


def local(p_vals, p_cols, f_cols):
    vals = p_vals.reshape(RB, 3, 2, BS, BS)
    left = vals.transpose(0, 1, 3, 2, 4).reshape(NT, BS, TW)
    right = vals.transpose(0, 1, 4, 2, 3).reshape(NT, BS, TW)
    keys = p_cols[:, 0]
    slot = jnp.arange(SLOT, dtype=jnp.int32)[None]
    place = jnp.arange(RB, dtype=jnp.int32)[:, None] * 3 + slot // 2
    hit = keys[:, None, :] == jnp.arange(32, dtype=jnp.int32)[None, :, None]
    lo = jnp.min(jnp.where(hit, (place + slot % 2 * NT)[:, None], 2 * NT), axis=2)
    hi = jnp.min(jnp.where(hit, (place + (1 - slot % 2) * NT)[:, None], 2 * NT), axis=2)
    row_data = jnp.concatenate([lo, hi, jnp.pad(keys, ((0, 0), (0, 64 - SLOT)))], axis=1)
    meta = jnp.concatenate([f_cols.reshape(RB, 128), row_data], axis=0)

    vm = pl.BlockSpec(memory_space=pltpu.VMEM)
    bf, f32 = jnp.bfloat16, jnp.float32
    out = pl.pallas_call(
        kernel,
        out_shape=jax.ShapeDtypeStruct((RB * NY, BS, TW), f32),
        in_specs=[vm] * 3,
        out_specs=vm,
        scratch_shapes=[
            pltpu.VMEM((4 * NY * NT, BS, TW), bf),
            pltpu.VMEM((8 * SEC, BS, TW), bf),
            pltpu.VMEM((SEC, BS, TW), bf),
            pltpu.VMEM((4 * NY, 8, 128), jnp.int32),
            pltpu.VMEM((8, 8, 128), jnp.int32),
            pltpu.SMEM((4 * NY, 8, 128), jnp.int32),
            pltpu.SMEM((8, 8, 128), jnp.int32),
            pltpu.SMEM((8, 128), jnp.int32),
            pltpu.VMEM((2, 4 * SLOT * BS, 2 * TW), bf),
            pltpu.VMEM((NY, RB * BS, TW), f32),
            pltpu.VMEM((NY, RB * BS, TW), bf),
            pltpu.VMEM((NY, RB * BS, TW), bf),
            pltpu.VMEM((NY, RB * BS, TW), bf),
            pltpu.VMEM((NY, RB * BS, TW), bf),
            pltpu.SemaphoreType.DMA((112,)),
            pltpu.SemaphoreType.DMA((4 * NY,)),
            pltpu.SemaphoreType.DMA((4 * NY,)),
            pltpu.SemaphoreType.DMA((8,)),
            pltpu.SemaphoreType.DMA((8,)),
            pltpu.SemaphoreType.DMA((NY,)),
            pltpu.SemaphoreType.DMA((NY,)),
            pltpu.SemaphoreType.DMA((NY,)),
            pltpu.SemaphoreType.DMA((NY,)),
            pltpu.SemaphoreType.DMA((3,)),
        ],
        compiler_params=pltpu.CompilerParams(
            collective_id=0, has_side_effects=True, vmem_limit_bytes=48 * 1024 * 1024),
    )(left, right, meta)
    out = out.reshape(RB, NY, BS // 2, 2, TW).transpose(0, 1, 3, 2, 4)
    return out.reshape(RB, 1, NY, 2, BS * BS)


def solution(mesh):
    return jax.shard_map(
        local,
        mesh=mesh,
        in_specs=(
            P(("row", "col"), "rep", None, None),
            P(("row", "col"), "rep", None),
            P(("row", "col"), None, None, None),
        ),
        out_specs=P(("row", "col"), "rep", None, None, None),
        check_vma=False,
    )
```

time: 498 us -> 92.8 us (0.19)
  local copies, waits for them, and re-layouts: 161 us -> 3.56 us
  waiting for transfers between devices: 145 us -> 0 us
  Pallas kernels: 0 us -> 88 us
  blocking collectives: 81.5 us -> 0 us
  matrix products: 74.1 us -> 0 us
  between operations: 13.5 us -> 0.08 us
  starting transfers between devices: 10.1 us -> 0 us
  other arithmetic: 7.51 us -> 0.96 us
    all_to_all x1 -> x0, waiting for transfers between devices: 96.8 us -> none  [local(): lax.all_to_all(outgoing, ('rep', 'col'), split_axis=1, concat_axis=1, til...]
    pallas_call x0 -> x1, Pallas kernels: none -> 88 us  [local(): pl.pallas_call(kernel, out_shape=jax.ShapeDtypeStruct((RB * NY, BS, TW),...]
    reshape x9 -> x6, local copies, waits for them, and re-layouts: 87.3 us -> 1.59 us  [the longest x3 1.13 us: local(): vals = p_vals.reshape(RB, 3, 2, BS, BS)]
    all_gather x3 -> x0, blocking collectives: 81.5 us -> none  [the longest x1 41.3 us: local(): lax.all_gather(own_cols, 'row', axis=0, tiled=True)]
    dot_general x9 -> x0, matrix products: 74.1 us -> none  [the longest x4 37.2 us: partial_block(): jnp.einsum('bsxy,bosky->boxk', left_blocks, right_blocks, preferred_eleme...]
    all_gather x2 -> x0, waiting for transfers between devices: 47.7 us -> none  [the longest x1 47.7 us: local(): lax.all_gather(own_vals, 'row', axis=0, tiled=True)]
    gather x8 -> x0, local copies, waits for them, and re-layouts: 35 us -> none  [the longest x4 32.4 us: partial_block(): picked = col_vals[wanted]]
    convert_element_type x3 -> x0, local copies, waits for them, and re-layouts: 30.5 us -> none  [local(): layer_terms = jnp.transpose(layers, (1, 2, 0, 3, 4)).astype(jnp.bfloat16)]
  transfers between devices with their start and end apart: 3 -> 0, of which waited for: 2 -> 0; matrix products, arithmetic and copies ran while one was open for 1% -> 0% of each run, Pallas kernels for 0% -> 0%
where the time goes in v2:
time: 92.8 us; the launch traced here: 92.6 us
  Pallas kernels  88 us (95%)
  local copies, waits for them, and re-layouts  3.56 us (4%)
  other arithmetic  0.96 us (1%)
    pallas_call x1, Pallas kernels, local(): pl.pallas_call(kernel, out_shape=jax.ShapeDtypeStruct((RB * NY, BS, TW),...  88 us

profile of v2, /device:TPU:1, one launch (start us, length us, event | category | flops | bytes accessed | tf_op | source)
XLA Modules:
  0.0 92.6 jit_solution(2023174767725677835)
XLA Ops:
  0.0 0.0 copy-start.1
  0.0 0.0 copy-start
  0.0 0.8 copy.16
  0.9 0.1 add_add_fusion
  0.9 0.1 select_reduce_fusion.1
  1.0 0.0 copy-done.1
  1.0 0.2 copy.15
  1.2 0.1 copy.17
  1.3 0.8 fusion.meta_ref
  2.1 0.0 copy-done
  2.1 0.4 reshape.151
  2.4 0.4 copy.14
  2.8 0.4 copy.20
  3.2 0.2 reshape.152.left_ref
  3.4 0.2 reshape.153.right_ref
  3.6 88.0 %shard_map.37 = f32[32,64,128]{2,1,0:T(8,128)S(1)} custom-call(bf16[12,64,128]{2,1,0:T(8,128)(2,1)S(1)} %reshape.152.left_ref, bf16[12,64,128]{2,1,0:T(8,128)(2,1)S(1)} %reshape.153.right_ref, s32[8,128]{1,0:T(8,128)S(1)} %fusion.meta_ref), custom_call_target="tpu_custom_call" | custom-call | tf_op jit(solution)/shard_map/pallas_call | solution.py:448
  91.6 1.0 %copy.22 = f32[4,1,8,2,4096]{4,3,2,1,0:T(2,128)} copy(f32[4,1,8,2,4096]{4,3,2,1,0:T(2,128)S(1)} %bitcast.13) | data formatting | bytes 2097152
  (3 shorter events, 0.0 us)
Async XLA Ops:
  0.0 1.0 %copy-start.1 = (s32[4,8,8,2]{2,3,1,0:T(2,128)S(1)}, s32[4,8,8,2]{2,3,1,0:T(2,128)}, u32[]{:S(2)}) copy-start(s32[4,8,8,2]{2,3,1,0:T(2,128)} %param.5) | copy-start | bytes 6148
  0.0 2.1 %copy-start = (bf16[4,1,6,4096]{3,0,2,1:T(4,128)(2,1)S(1)}, bf16[4,1,6,4096]{3,0,2,1:T(4,128)(2,1)}, u32[]{:S(2)}) copy-start(bf16[4,1,6,4096]{3,0,2,1:T(4,128)(2,1)} %param.3) | copy-start | bytes 589828

commit v3 on v2

--- a/solution.py
+++ b/solution.py
@@ -88,8 +88,8 @@
     def lslot(yy, c, q):
         return (yy * 2 + c) * 2 + q
 
-    def ltiles(s):
-        return lbuf.at[pl.ds(s * NT, NT)]
+    def ltiles(s, h):
+        return lbuf.at[pl.ds(s * NT + h * (NT // 2), NT // 2)]
 
     def rtiles(s):
         return rtab.at[pl.ds(s * SEC, NT)]
@@ -116,12 +116,14 @@
         for c in near_copies():
             c.start()
 
-    def lsend(src, msrc, slot, to):
-        send(src, ltiles(slot), lr.at[slot], to)
-        send(msrc, lmv.at[slot], lmr.at[slot], to)
-
-    for to in (z_next, up, down, sibling):
-        lsend(left_ref, meta_ref, own, to)
+    def lsend_own(to):
+        for h in range(2):
+            send(left_ref.at[pl.ds(h * (NT // 2), NT // 2)], ltiles(own, h), lr.at[own, h], to)
+            if h == 0:
+                send(meta_ref, lmv.at[own], lmr.at[own], to)
+
+    for to in (up, down, sibling):
+        lsend_own(to)
 
     order = [(core, zp), (other, zp), (core, 1 - zp), (other, 1 - zp)]
     base_mark = take(16)
@@ -166,33 +168,35 @@
         otab[i] = v
         otab[NT + i] = swap(v)
 
-    def larrive(slot):
-        arrive(ltiles(slot), lr.at[slot])
-        arrive(lmv.at[slot], lmr.at[slot])
-
-    def lpass(slot, to):
-        lsend(ltiles(slot), lmv.at[slot], slot, to)
-
-    marks = {1: take(16), 2: take(16), 3: take(12), 4: take(4)}
-
-    def lring(s):
+    def larrive(slot, h):
+        arrive(ltiles(slot, h), lr.at[slot, h])
+        if h == 0:
+            arrive(lmv.at[slot], lmr.at[slot])
+
+    marks = {1: take(32), 2: take(32), 3: take(24), 4: take(8)}
+
+    def lring(s, part=None):
         i = marks[s]
-        for q, half in ((zp, 0), (1 - zp, 1)):
-            for yy, to, way in (((y + NY - s) % NY, up, 0), ((y + s) % NY, down, 1)):
-                if s == 4 and way == 1:
-                    continue
-                slot = lslot(yy, core, q)
-                goals = [to] if s < 3 or (s == 3 and half == way) else []
-                copies = []
-                for goal in goals + [sibling]:
-                    copies.append(describe(i, ltiles(slot), ltiles(slot), lr.at[slot], goal))
-                    copies.append(describe(i + 1, lmv.at[slot], lmv.at[slot], lmr.at[slot], goal))
-                    i += 2
-                yield slot, copies
-
-    def lstep(s):
-        for slot, copies in lring(s):
-            larrive(slot)
+        for q, tile in ((zp, 0), (1 - zp, 1)):
+            for h in range(2):
+                for yy, to, way in (((y + NY - s) % NY, up, 0), ((y + s) % NY, down, 1)):
+                    if s == 4 and way != h:
+                        continue
+                    slot = lslot(yy, core, q)
+                    goals = [to] if s < 3 or (s == 3 and h == way) else []
+                    copies = []
+                    for goal in goals + [sibling]:
+                        if part is None or tile == part:
+                            copies.append(describe(i, ltiles(slot, h), ltiles(slot, h), lr.at[slot, h], goal))
+                            if h == 0:
+                                copies.append(describe(i + 1, lmv.at[slot], lmv.at[slot], lmr.at[slot], goal))
+                        i += 2
+                    if copies:
+                        yield h, slot, copies
+
+    def lstep(s, part=None):
+        for h, slot, copies in lring(s, part):
+            larrive(slot, h)
             for c in copies:
                 c.start()
 
@@ -214,50 +218,79 @@
     no_base = jnp.logical_not(is_base)
     differs = jnp.logical_not(same)
 
+    def last_right():
+        @pl.when(is_base)
+        def _():
+            for k in range(4):
+                rarrive(rsec((x + 2) % NX, *order[k]))
+
+        @pl.when(no_base)
+        def _():
+            for k in range(4):
+                rarrive(rsec(xp if k % 2 == 0 else xm, *order[k]))
+
+    def pair_on():
+        for h in range(2):
+            larrive(pair, h)
+            for c in pair_copies(h):
+                c.start()
+
+    pair = lslot(y, core, 1 - zp)
+    pair_mark = take(12)
+
+    def pair_copies(h):
+        i = pair_mark + 6 * h
+        for to in (up, down, sibling):
+            yield describe(i, ltiles(pair, h), ltiles(pair, h), lr.at[pair, h], to)
+            if h == 0:
+                yield describe(i + 1, lmv.at[pair], lmv.at[pair], lmr.at[pair], to)
+            i += 2
+
     @pl.when(keeps_own)
     def _():
         base((1, 2, 3))
 
-    pair = lslot(y, core, 1 - zp)
-    larrive(pair)
-    for to in (up, down, sibling):
-        lpass(pair, to)
+    lstep(1, 0)
+    lsend_own(z_next)
+
+    @pl.when(jnp.logical_and(no_base, same))
+    def _():
+        hop_on((0, 1))
+
+    lstep(2, 0)
+
+    @pl.when(jnp.logical_and(no_base, same))
+    def _():
+        hop_on((2, 3))
 
     @pl.when(jnp.logical_and(is_base, differs))
     def _():
         base((0, 1, 2, 3))
 
-    @pl.when(jnp.logical_and(no_base, same))
-    def _():
-        hop_on((0, 1, 2, 3))
-
-    lstep(1)
-
-    @pl.when(jnp.logical_and(no_base, differs))
-    def _():
-        hop_on((0, 1))
+    lstep(3, 0)
+    pair_on()
+
+    @pl.when(same)
+    def _():
+        last_right()
 
     @pl.when(differs)
     def _():
-        lstep(2)
-
-    @pl.when(jnp.logical_and(no_base, differs))
-    def _():
-        hop_on((2, 3))
-
-    @pl.when(no_base)
-    def _():
-        for k in range(4):
-            rarrive(rsec(xp if k % 2 == 0 else xm, *order[k]))
-
-    @pl.when(is_base)
-    def _():
-        for k in range(4):
-            rarrive(rsec((x + 2) % NX, *order[k]))
+        @pl.when(no_base)
+        def _():
+            hop_on((0, 1))
+        lstep(1, 1)
+
+        @pl.when(no_base)
+        def _():
+            hop_on((2, 3))
+        lstep(2, 1)
+        lstep(3, 1)
+        last_right()
 
     rm_copy = pltpu.make_async_copy(rmv, rms, msem.at[0])
     rm_copy.start()
-    om_copy = pltpu.make_async_copy(meta_ref, oms, msem.at[2])
+    om_copy = pltpu.make_async_copy(meta_ref, oms, msem.at[3])
     om_copy.start()
 
     def widen(sec, carry):
@@ -276,7 +309,7 @@
 
     def meta_copy(n):
         g = group_of(n)
-        return pltpu.make_async_copy(lmv.at[pl.ds(g * 4, 4)], lms.at[pl.ds(g * 4, 4)], msem.at[1])
+        return pltpu.make_async_copy(lmv.at[pl.ds(g * 4, 4)], lms.at[pl.ds(g * 4, 4)], msem.at[1 + n % 2])
 
     def meta_in(n):
         g = group_of(n)
@@ -289,7 +322,8 @@
         g = group_of(n)
         for q in range(2):
             slot = lslot(g, other, q)
-            arrive(ltiles(slot), lr.at[slot])
+            for h in range(2):
+                arrive(ltiles(slot, h), lr.at[slot, h])
         dests = (zl, zf)
         for rb in range(RB):
             tiles = [lbuf[(g * 4 + t) * NT + rb * 3 + p] for t in range(4) for p in range(3)]
@@ -362,24 +396,24 @@
     def main(n, carry):
         @pl.when(n < NY)
         def _():
-            meta_copy(n).wait()
-
-            @pl.when(jnp.logical_and(n == 1, same))
-            def _():
-                lstep(2)
-
-            @pl.when(n == 3)
-            def _():
-                lstep(3)
-
-            @pl.when(n == 5)
+            for s in range(1, 4):
+                @pl.when(jnp.logical_and(n == 2 * s - 1, same))
+                def _(s=s):
+                    lstep(s, 1)
+
+            @pl.when(n == jnp.where(same, 7, 1))
             def _():
                 lstep(4)
 
-            @pl.when(n < NY - 1)
+            @pl.when(n % 2 == 1)
             def _():
-                meta_in(n + 1)
-
+                meta_in(n)
+
+                @pl.when(n < NY - 1)
+                def _():
+                    meta_in(n + 1)
+
+            meta_copy(n).wait()
             compute(n)
             zcopy(n).start()
 
@@ -396,8 +430,11 @@
 
     for c in sent:
         describe(*c).wait_send()
+    for h in range(2):
+        for c in pair_copies(h):
+            c.wait_send()
     for s in range(1, 5):
-        for slot, copies in lring(s):
+        for h, slot, copies in lring(s):
             for c in copies:
                 c.wait_send()
 
@@ -465,8 +502,8 @@
             pltpu.VMEM((NY, RB * BS, TW), bf),
             pltpu.VMEM((NY, RB * BS, TW), bf),
             pltpu.VMEM((NY, RB * BS, TW), bf),
-            pltpu.SemaphoreType.DMA((112,)),
-            pltpu.SemaphoreType.DMA((4 * NY,)),
+            pltpu.SemaphoreType.DMA((176,)),
+            pltpu.SemaphoreType.DMA((4 * NY, 2)),
             pltpu.SemaphoreType.DMA((4 * NY,)),
             pltpu.SemaphoreType.DMA((8,)),
             pltpu.SemaphoreType.DMA((8,)),
@@ -474,7 +511,7 @@
             pltpu.SemaphoreType.DMA((NY,)),
             pltpu.SemaphoreType.DMA((NY,)),
             pltpu.SemaphoreType.DMA((NY,)),
-            pltpu.SemaphoreType.DMA((3,)),
+            pltpu.SemaphoreType.DMA((4,)),
         ],
         compiler_params=pltpu.CompilerParams(
             collective_id=0, has_side_effects=True, vmem_limit_bytes=48 * 1024 * 1024),

time: 92.8 us -> 88.4 us (0.953)
  Pallas kernels: 88 us -> 82.9 us
    pallas_call x1, Pallas kernels: 88 us -> 82.9 us  [local(): pl.pallas_call(kernel, out_shape=jax.ShapeDtypeStruct((RB * NY, BS, TW),...]
where the time goes in v3:
time: 88.4 us; the launch traced here: 87.5 us
  Pallas kernels  82.9 us (94%)
  local copies, waits for them, and re-layouts  3.56 us (4%)
  other arithmetic  0.96 us (1%)
    pallas_call x1, Pallas kernels, local(): pl.pallas_call(kernel, out_shape=jax.ShapeDtypeStruct((RB * NY, BS, TW),...  82.9 us

profile of v3, /device:TPU:1, one launch (start us, length us, event | category | flops | bytes accessed | tf_op | source)
XLA Modules:
  0.0 87.5 jit_solution(13871953538738909023)
XLA Ops:
  0.0 0.0 copy-start.1
  0.0 0.0 copy-start
  0.0 0.8 copy.16
  0.9 0.1 add_add_fusion
  0.9 0.1 select_reduce_fusion.1
  1.0 0.0 copy-done.1
  1.0 0.2 copy.15
  1.2 0.1 copy.17
  1.3 0.8 fusion.meta_ref
  2.1 0.0 copy-done
  2.1 0.4 reshape.151
  2.4 0.4 copy.14
  2.8 0.4 copy.20
  3.2 0.2 reshape.152.left_ref
  3.4 0.2 reshape.153.right_ref
  3.6 82.9 %shard_map.37 = f32[32,64,128]{2,1,0:T(8,128)S(1)} custom-call(bf16[12,64,128]{2,1,0:T(8,128)(2,1)S(1)} %reshape.152.left_ref, bf16[12,64,128]{2,1,0:T(8,128)(2,1)S(1)} %reshape.153.right_ref, s32[8,128]{1,0:T(8,128)S(1)} %fusion.meta_ref), custom_call_target="tpu_custom_call" | custom-call | tf_op jit(solution)/shard_map/pallas_call | solution.py:485
  86.5 1.0 %copy.22 = f32[4,1,8,2,4096]{4,3,2,1,0:T(2,128)} copy(f32[4,1,8,2,4096]{4,3,2,1,0:T(2,128)S(1)} %bitcast.13) | data formatting | bytes 2097152
  (3 shorter events, 0.0 us)
Async XLA Ops:
  0.0 1.0 %copy-start.1 = (s32[4,8,8,2]{2,3,1,0:T(2,128)S(1)}, s32[4,8,8,2]{2,3,1,0:T(2,128)}, u32[]{:S(2)}) copy-start(s32[4,8,8,2]{2,3,1,0:T(2,128)} %param.5) | copy-start | bytes 6148
  0.0 2.1 %copy-start = (bf16[4,1,6,4096]{3,0,2,1:T(4,128)(2,1)S(1)}, bf16[4,1,6,4096]{3,0,2,1:T(4,128)(2,1)}, u32[]{:S(2)}) copy-start(bf16[4,1,6,4096]{3,0,2,1:T(4,128)(2,1)} %param.3) | copy-start | bytes 589828

commit v4 on v3

--- a/solution.py
+++ b/solution.py
@@ -17,7 +17,7 @@
 NY = 8
 RB = 4
 SLOT = 6
-LAG = 2
+LAG = 3
 
 
 def kernel(left_ref, right_ref, meta_ref, out_ref,
@@ -263,28 +263,29 @@
     def _():
         hop_on((2, 3))
 
-    @pl.when(jnp.logical_and(is_base, differs))
-    def _():
-        base((0, 1, 2, 3))
-
     lstep(3, 0)
     pair_on()
 
+    @pl.when(jnp.logical_and(is_base, differs))
+    def _():
+        base((0, 1, 2, 3))
+
     @pl.when(same)
     def _():
         last_right()
 
     @pl.when(differs)
     def _():
+        lstep(1, 1)
+
         @pl.when(no_base)
         def _():
             hop_on((0, 1))
-        lstep(1, 1)
+        lstep(2, 1)
 
         @pl.when(no_base)
         def _():
             hop_on((2, 3))
-        lstep(2, 1)
         lstep(3, 1)
         last_right()
 

time: 88.4 us -> 84.3 us (0.954)
  Pallas kernels: 82.9 us -> 79.3 us
    pallas_call x1, Pallas kernels: 82.9 us -> 79.3 us  [local(): pl.pallas_call(kernel, out_shape=jax.ShapeDtypeStruct((RB * NY, BS, TW),...]
where the time goes in v4:
time: 84.3 us; the launch traced here: 83.9 us
  Pallas kernels  79.3 us (94%)
  local copies, waits for them, and re-layouts  3.56 us (4%)
  other arithmetic  0.96 us (1%)
    pallas_call x1, Pallas kernels, local(): pl.pallas_call(kernel, out_shape=jax.ShapeDtypeStruct((RB * NY, BS, TW),...  79.3 us

profile of v4, /device:TPU:1, one launch (start us, length us, event | category | flops | bytes accessed | tf_op | source)
XLA Modules:
  0.0 83.9 jit_solution(9816514272605111886)
XLA Ops:
  0.0 0.0 copy-start.1
  0.0 0.0 copy-start
  0.0 0.8 copy.16
  0.9 0.1 add_add_fusion
  0.9 0.1 select_reduce_fusion.1
  1.0 0.0 copy-done.1
  1.0 0.2 copy.15
  1.2 0.1 copy.17
  1.3 0.8 fusion.meta_ref
  2.1 0.0 copy-done
  2.1 0.4 reshape.151
  2.4 0.4 copy.14
  2.8 0.4 copy.20
  3.2 0.2 reshape.152.left_ref
  3.4 0.2 reshape.153.right_ref
  3.6 79.3 %shard_map.37 = f32[32,64,128]{2,1,0:T(8,128)S(1)} custom-call(bf16[12,64,128]{2,1,0:T(8,128)(2,1)S(1)} %reshape.152.left_ref, bf16[12,64,128]{2,1,0:T(8,128)(2,1)S(1)} %reshape.153.right_ref, s32[8,128]{1,0:T(8,128)S(1)} %fusion.meta_ref), custom_call_target="tpu_custom_call" | custom-call | tf_op jit(solution)/shard_map/pallas_call | solution.py:486
  82.9 1.0 %copy.22 = f32[4,1,8,2,4096]{4,3,2,1,0:T(2,128)} copy(f32[4,1,8,2,4096]{4,3,2,1,0:T(2,128)S(1)} %bitcast.13) | data formatting | bytes 2097152
  (3 shorter events, 0.0 us)
Async XLA Ops:
  0.0 1.0 %copy-start.1 = (s32[4,8,8,2]{2,3,1,0:T(2,128)S(1)}, s32[4,8,8,2]{2,3,1,0:T(2,128)}, u32[]{:S(2)}) copy-start(s32[4,8,8,2]{2,3,1,0:T(2,128)} %param.5) | copy-start | bytes 6148
  0.0 2.1 %copy-start = (bf16[4,1,6,4096]{3,0,2,1:T(4,128)(2,1)S(1)}, bf16[4,1,6,4096]{3,0,2,1:T(4,128)(2,1)}, u32[]{:S(2)}) copy-start(bf16[4,1,6,4096]{3,0,2,1:T(4,128)(2,1)} %param.3) | copy-start | bytes 589828

commit v5 on v4

--- a/solution.py
+++ b/solution.py
@@ -17,7 +17,7 @@
 NY = 8
 RB = 4
 SLOT = 6
-LAG = 3
+LAG = 4
 
 
 def kernel(left_ref, right_ref, meta_ref, out_ref,

time: 84.3 us -> 83.6 us (level)
  no operation moved by 1% of the time
where the time goes in v5:
time: 83.6 us; the launch traced here: 83.5 us
  Pallas kernels  78.9 us (94%)
  local copies, waits for them, and re-layouts  3.56 us (4%)
  other arithmetic  0.96 us (1%)
    pallas_call x1, Pallas kernels, local(): pl.pallas_call(kernel, out_shape=jax.ShapeDtypeStruct((RB * NY, BS, TW),...  78.9 us

profile of v5, /device:TPU:1, one launch (start us, length us, event | category | flops | bytes accessed | tf_op | source)
XLA Modules:
  0.0 83.5 jit_solution(8823253419799464117)
XLA Ops:
  0.0 0.0 copy-start.1
  0.0 0.0 copy-start
  0.0 0.8 copy.16
  0.9 0.1 add_add_fusion
  0.9 0.1 select_reduce_fusion.1
  1.0 0.0 copy-done.1
  1.0 0.2 copy.15
  1.2 0.1 copy.17
  1.3 0.8 fusion.meta_ref
  2.1 0.0 copy-done
  2.1 0.4 reshape.151
  2.4 0.4 copy.14
  2.8 0.4 copy.20
  3.2 0.2 reshape.152.left_ref
  3.4 0.2 reshape.153.right_ref
  3.6 78.9 %shard_map.37 = f32[32,64,128]{2,1,0:T(8,128)S(1)} custom-call(bf16[12,64,128]{2,1,0:T(8,128)(2,1)S(1)} %reshape.152.left_ref, bf16[12,64,128]{2,1,0:T(8,128)(2,1)S(1)} %reshape.153.right_ref, s32[8,128]{1,0:T(8,128)S(1)} %fusion.meta_ref), custom_call_target="tpu_custom_call" | custom-call | tf_op jit(solution)/shard_map/pallas_call | solution.py:486
  82.5 1.0 %copy.22 = f32[4,1,8,2,4096]{4,3,2,1,0:T(2,128)} copy(f32[4,1,8,2,4096]{4,3,2,1,0:T(2,128)S(1)} %bitcast.13) | data formatting | bytes 2097152
  (3 shorter events, 0.0 us)
Async XLA Ops:
  0.0 1.0 %copy-start.1 = (s32[4,8,8,2]{2,3,1,0:T(2,128)S(1)}, s32[4,8,8,2]{2,3,1,0:T(2,128)}, u32[]{:S(2)}) copy-start(s32[4,8,8,2]{2,3,1,0:T(2,128)} %param.5) | copy-start | bytes 6148
  0.0 2.1 %copy-start = (bf16[4,1,6,4096]{3,0,2,1:T(4,128)(2,1)S(1)}, bf16[4,1,6,4096]{3,0,2,1:T(4,128)(2,1)}, u32[]{:S(2)}) copy-start(bf16[4,1,6,4096]{3,0,2,1:T(4,128)(2,1)} %param.3) | copy-start | bytes 589828

commit v6 on v5

--- a/solution.py
+++ b/solution.py
@@ -406,7 +406,7 @@
             def _():
                 lstep(4)
 
-            @pl.when(n % 2 == 1)
+            @pl.when(jnp.logical_and(n % 2 == 1, same))
             def _():
                 meta_in(n)
 
@@ -415,6 +415,15 @@
                     meta_in(n + 1)
 
             meta_copy(n).wait()
+
+            @pl.when(jnp.logical_and(n % 2 == 0, differs))
+            def _():
+                meta_in(n + 1)
+
+                @pl.when(n < NY - 2)
+                def _():
+                    meta_in(n + 2)
+
             compute(n)
             zcopy(n).start()
 

time: 83.6 us -> 83.9 us (level)
  no operation moved by 1% of the time
where the time goes in v6:
time: 83.9 us; the launch traced here: 83.7 us
  Pallas kernels  79.1 us (94%)
  local copies, waits for them, and re-layouts  3.56 us (4%)
  other arithmetic  0.96 us (1%)
    pallas_call x1, Pallas kernels, local(): pl.pallas_call(kernel, out_shape=jax.ShapeDtypeStruct((RB * NY, BS, TW),...  79.1 us

profile of v6, /device:TPU:1, one launch (start us, length us, event | category | flops | bytes accessed | tf_op | source)
XLA Modules:
  0.0 83.7 jit_solution(8289459258641472310)
XLA Ops:
  0.0 0.0 copy-start.1
  0.0 0.0 copy-start
  0.0 0.8 copy.16
  0.9 0.1 add_add_fusion
  0.9 0.1 select_reduce_fusion.1
  1.0 0.0 copy-done.1
  1.0 0.2 copy.15
  1.2 0.1 copy.17
  1.3 0.8 fusion.meta_ref
  2.1 0.0 copy-done
  2.1 0.4 reshape.151
  2.4 0.4 copy.14
  2.8 0.4 copy.20
  3.2 0.2 reshape.152.left_ref
  3.4 0.2 reshape.153.right_ref
  3.6 79.1 %shard_map.37 = f32[32,64,128]{2,1,0:T(8,128)S(1)} custom-call(bf16[12,64,128]{2,1,0:T(8,128)(2,1)S(1)} %reshape.152.left_ref, bf16[12,64,128]{2,1,0:T(8,128)(2,1)S(1)} %reshape.153.right_ref, s32[8,128]{1,0:T(8,128)S(1)} %fusion.meta_ref), custom_call_target="tpu_custom_call" | custom-call | tf_op jit(solution)/shard_map/pallas_call | solution.py:495
  82.7 1.0 %copy.22 = f32[4,1,8,2,4096]{4,3,2,1,0:T(2,128)} copy(f32[4,1,8,2,4096]{4,3,2,1,0:T(2,128)S(1)} %bitcast.13) | data formatting | bytes 2097152
  (3 shorter events, 0.0 us)
Async XLA Ops:
  0.0 1.0 %copy-start.1 = (s32[4,8,8,2]{2,3,1,0:T(2,128)S(1)}, s32[4,8,8,2]{2,3,1,0:T(2,128)}, u32[]{:S(2)}) copy-start(s32[4,8,8,2]{2,3,1,0:T(2,128)} %param.5) | copy-start | bytes 6148
  0.0 2.1 %copy-start = (bf16[4,1,6,4096]{3,0,2,1:T(4,128)(2,1)S(1)}, bf16[4,1,6,4096]{3,0,2,1:T(4,128)(2,1)}, u32[]{:S(2)}) copy-start(bf16[4,1,6,4096]{3,0,2,1:T(4,128)(2,1)} %param.3) | copy-start | bytes 589828
